TPU v7x, 512 devices: a whole 4x8x8 slice. The times are simulated.
512 devices in a mesh: dp: 16 (over x, z_lo, core), ctx: 32 (over z_hi, y).
Axes of the slice: x: 4, y: 8, z: 8 (z_hi: 4, z_lo: 2; z = z_hi * 2 + z_lo), core: 2. Of those that a mesh axis runs over, the one named last changes fastest.
Arguments:
- queries: bfloat16 [16, 4096, 1024], P('dp', 'ctx'), may hold values from -60 to 60
- keys: bfloat16 [16, 4096, 128], P('dp', 'ctx'), may hold values from -6 to 6
- values: bfloat16 [16, 4096, 192], P('dp', 'ctx'), may hold values from -96 to 96
- features_fine: bfloat16 [16, 8192, 1536], P('dp', 'ctx'), may hold values from -6 to 6
- rc_state: bfloat16 [16, 4096, 1536], P('dp', 'ctx'), may hold values from -6 to 6
- conv_weight: float32 [5, 1536], replicated, may hold values from -2.5 to 2.5
Outputs:
- d_fine: bfloat16 [16, 8192, 1536], P('dp', 'ctx')
- d_weight: float32 [5, 1536], replicated
All inputs are finite; a program needn't handle non-finite values.
Results may differ from a plain program's by a relative error of at most 0.0085.
Values may be sent and summed in bfloat16 or wider, within the bound.
A program may use at most 64 MiB of HBM per device.

v0:
```python
import math
import jax
import jax.numpy as jnp
from jax import lax
from jax.sharding import PartitionSpec as P

HEADS = 8
KW = 5


def padded_2(cells, sides, width):
    for axis, dim in sides:
        count = lax.axis_size(axis)
        ends = count - 1
        head = lax.slice_in_dim(cells, 0, width, axis=dim)
        tail = lax.slice_in_dim(cells, cells.shape[dim] - width, cells.shape[dim], axis=dim)
        cells = jnp.concatenate(
            [
                lax.ppermute(tail, axis, [(i, (i + 1) % count) for i in range(ends)]),
                cells,
                lax.ppermute(head, axis, [((i + 1) % count, i) for i in range(ends)]),
            ],
            axis=dim,
        )
    return cells


def body(queries, keys, values, features_fine, rc_state, conv_weight):
    tok_rows = queries.shape[1]
    key_size = keys.shape[2]
    value_size = values.shape[2]
    q_heads = queries[0].reshape(tok_rows, HEADS, key_size)
    ctx_count = lax.axis_size("ctx")
    run_top = jnp.full((tok_rows, HEADS), -1e30, jnp.float32)
    key_piece = lax.all_gather(keys, "ctx", axis=1, tiled=True)
    value_piece = lax.all_gather(values, "ctx", axis=1, tiled=True)
    scores = jnp.einsum(
        "qhd,kd->qhk", q_heads, key_piece[0], preferred_element_type=jnp.float32
    ) * key_size ** (-0.5)
    new_top = jnp.maximum(run_top, jnp.max(scores, axis=-1))
    expd = jnp.exp(scores - new_top[..., None])
    new_total = jnp.sum(expd, axis=-1)
    mixed = jnp.einsum(
        "qhk,kv->qhv", expd.astype(jnp.bfloat16), value_piece[0], preferred_element_type=jnp.float32
    )
    attended = (mixed / new_total[..., None]).reshape(tok_rows, HEADS * value_size)[None]
    padded = padded_2(features_fine, (("ctx", 1),), 2)
    taps = [padded[:, k : k + 2 * tok_rows : 2, :].astype(jnp.float32) for k in range(KW)]
    coarse = conv_weight[0] * taps[0]
    for k in range(1, KW):
        coarse = coarse + conv_weight[k] * taps[k]
    slices = lax.all_to_all(rc_state, "ctx", split_axis=2, concat_axis=0, tiled=True)
    flipped = slices[::-1]
    mirrored = lax.all_to_all(flipped, "ctx", split_axis=0, concat_axis=2, tiled=True)
    grad = coarse + attended - mirrored[:, ::-1, :].astype(jnp.float32)
    gpad = padded_2(grad.astype(jnp.bfloat16), (("ctx", 1),), 1).astype(grad.dtype)
    even = (
        conv_weight[0] * gpad[:, 2:]
        + conv_weight[2] * gpad[:, 1:-1]
        + conv_weight[4] * gpad[:, :-2]
    )
    odd = conv_weight[1] * gpad[:, 2:] + conv_weight[3] * gpad[:, 1:-1]
    d_fine = (
        jnp.stack([even, odd], axis=2)
        .reshape(grad.shape[0], 2 * tok_rows, grad.shape[2])
        .astype(jnp.bfloat16)
    )
    partial_grad = jnp.stack([jnp.sum(grad * taps[k], axis=(0, 1)) for k in range(KW)])
    summed = lax.psum(partial_grad, ("dp", "ctx"))
    scale = 1.0 / math.sqrt(lax.axis_size("dp") * tok_rows * ctx_count)
    return (d_fine, summed * scale)


def solution(mesh):
    placed = (
        P("dp", "ctx", None),
        P("dp", "ctx", None),
        P("dp", "ctx", None),
        P("dp", "ctx", None),
        P("dp", "ctx", None),
        P(),
    )
    return jax.shard_map(
        body, mesh=mesh, in_specs=placed, out_specs=(P("dp", "ctx", None), P()), check_vma=False
    )
```

profile of v0, /device:TPU:184, one launch (start us, length us, event | category | flops | bytes accessed | tf_op | source)
XLA Modules:
  0.0 341.5 jit_solution(18383458230890813925)
XLA Ops:
  7.2 0.0 all-gather.3.cloned.1.call-start
  7.2 0.7 all-gather.3.cloned.1.call-update
  7.9 2.2 copy.29
  10.1 0.5 broadcast.15
  10.6 8.8 %reduce.10 = bf16[1536,128]{1,0:T(8,128)(2,1)S(1)} reduce(bf16[1536,1,128]{2,1,0:T(2,128)(2,1)S(1)} %bitcast.34, bf16[]{:T(256)} %broadcast.15), dimensions={1}, to_apply=%bitcast.29.reduce_sub_computation | reduce | bytes 786434
  19.4 0.8 reshape.84
  20.2 13.8 %all-to-all-start = ((bf16[32,2,3072]{2,1,0:T(2,128)(2,1)}), bf16[32,2,3072]{2,1,0:T(2,128)(2,1)S(1)}, u32[]{:S(2)}, u32[]{:S(2)}) async-start(bf16[32,2,3072]{2,1,0:T(2,128)(2,1)} %reshape.84), calls=%async_computation | async-start | bytes 786432 | tf_op jit(solution)/shard_map/all_to_all | solution.py:52
  34.0 0.0 all-gather.5.cloned.1.call-start
  34.1 0.7 all-gather.5.cloned.1.call-update
  34.8 12.8 %all-to-all-done = bf16[32,2,3072]{2,1,0:T(2,128)(2,1)S(1)} async-done(((bf16[32,2,3072]{2,1,0:T(2,128)(2,1)}), bf16[32,2,3072]{2,1,0:T(2,128)(2,1)S(1)}, u32[]{:S(2)}, u32[]{:S(2)}) %all-to-all-start) | async-done | bytes 393248 | tf_op jit(solution)/shard_map/all_to_all | solution.py:52
  47.6 0.3 reshape.85
  47.9 0.1 copy.31
  48.0 0.8 rev.6
  48.7 8.5 %all-to-all-start.1 = ((bf16[32,128,48]{1,2,0:T(8,128)(2,1)}), bf16[32,128,48]{1,2,0:T(8,128)(2,1)S(1)}, u32[]{:S(2)}, u32[]{:S(2)}) async-start(bf16[32,128,48]{1,2,0:T(8,128)(2,1)} %rev.6), calls=%async_computation.1 | async-start | bytes 786432 | tf_op jit(solution)/shard_map/all_to_all | solution.py:54
  57.3 0.3 copy.24
  57.5 5.5 %collective-permute-start = (bf16[1,2,1536]{1,2,0:T(8,128)(2,1)S(1)}, bf16[1,2,1536]{1,2,0:T(8,128)(2,1)}, u32[]{:S(2)}, u32[]{:S(2)}) collective-permute-start(bf16[1,2,1536]{1,2,0:T(8,128)(2,1)S(1)} %copy.24), channel_id=1, source_target_pairs={{0,1},{1,2},{2,3},{3,4},{4,5},{5,6},{6,7},{7,8},{8,9},{9,10},{10,1... | collective-permute-start | bytes 18440 | tf_op jit(solution)/shard_map/ppermute | solution.py:19
  63.0 0.3 copy.25
  63.3 2.1 collective-permute-start.1
  65.4 0.1 slice_reduce_fusion.4
  65.5 0.3 copy.26
  65.8 1.0 copy.32
  66.8 14.4 %slice.65 = bf16[1,128,1536]{1,2,0:T(8,128)(2,1)S(1)} slice(bf16[1,256,1536]{1,2,0:T(8,128)(2,1)S(1)} %copy.26), slice={[0:1:1], [0:256:2], [0:1536:1]} | slice | bytes 786432 | tf_op jit(solution)/shard_map/slice | solution.py:48
  81.2 5.9 %collective-permute-done.1 = bf16[1,2,1536]{1,2,0:T(8,128)(2,1)} collective-permute-done((bf16[1,2,1536]{1,2,0:T(8,128)(2,1)S(1)}, bf16[1,2,1536]{1,2,0:T(8,128)(2,1)}, u32[]{:S(2)}, u32[]{:S(2)}) %collective-permute-start.1) | collective-permute-done | bytes 6176 | tf_op jit(solution)/shard_map/ppermute | solution.py:21
  87.1 1.8 pad_maximum_fusion
  88.9 14.4 %slice.61 = bf16[1,128,1536]{1,2,0:T(8,128)(2,1)S(1)} slice(bf16[1,260,1536]{1,2,0:T(8,128)(2,1)S(1)} %pad_maximum_fusion), slice={[0:1:1], [0:256:2], [0:1536:1]} | slice | bytes 786432 | tf_op jit(solution)/shard_map/slice | solution.py:48
  103.3 14.4 %slice.63 = bf16[1,128,1536]{1,2,0:T(8,128)(2,1)S(1)} slice(bf16[1,260,1536]{1,2,0:T(8,128)(2,1)S(1)} %pad_maximum_fusion), slice={[0:1:1], [1:257:2], [0:1536:1]} | slice | bytes 786432 | tf_op jit(solution)/shard_map/slice | solution.py:48
  117.7 14.7 %slice.67 = bf16[1,128,1536]{1,2,0:T(8,128)(2,1)S(1)} slice(bf16[1,260,1536]{1,2,0:T(8,128)(2,1)S(1)} %pad_maximum_fusion), slice={[0:1:1], [3:259:2], [0:1536:1]} | slice | bytes 786432 | tf_op jit(solution)/shard_map/slice | solution.py:48
  132.4 15.0 %slice.69 = bf16[1,128,1536]{1,2,0:T(8,128)(2,1)} slice(bf16[1,260,1536]{1,2,0:T(8,128)(2,1)S(1)} %pad_maximum_fusion), slice={[0:1:1], [4:260:2], [0:1536:1]} | slice | bytes 786432 | tf_op jit(solution)/shard_map/slice | solution.py:48
  147.4 1.3 rev.7
  148.7 0.0 all-gather.3.cloned.1.call-done
  148.8 9.3 %multiply_reduce_fusion = (f32[128,8]{0,1:T(8,128)S(1)}, f32[128,8,4096]{2,0,1:T(8,128)}) fusion(bf16[1,4096,128]{2,1,0:T(8,128)(2,1)} %all-gather.3.cloned.1.call-done, bf16[128,8,128]{2,1,0:T(8,128)(2,1)S(1)} %bitcast.36), kind=kOutput, calls=%fused_computation.1 | convolution fusion | flops 1082129408 | bytes 18092032 | tf_op jit(solution)/shard_map/qhd,kd->qhk/dot_general | solution.py:37
  158.0 8.6 %fusion = f32[128,8]{0,1:T(8,128)S(1)} fusion(f32[128,8,4096]{2,0,1:T(8,128)} %get-tuple-element.20, f32[128,8]{0,1:T(8,128)S(1)} %broadcast_maximum_fusion), kind=kLoop, calls=%fused_computation.2 | loop fusion | flops 12581888 | bytes 16785408 | tf_op jit(solution)/shard_map/reduce_sum | solution.py:42
  166.7 29.0 %all-gather.5.cloned.1.call-done = bf16[1,4096,192]{1,2,0:T(8,128)(2,1)} async-done(((bf16[1,128,192]{1,2,0:T(8,128)(2,1)}), bf16[1,4096,192]{1,2,0:T(8,128)(2,1)}) %all-gather.5.cloned.1.call-update) | async-done | bytes 1572880 | tf_op jit(solution)/shard_map/all_gather | solution.py:36
  195.6 8.0 %fusion.7 = f32[128,8,192]{0,2,1:T(8,128)S(1)} fusion(bf16[1,4096,192]{1,2,0:T(8,128)(2,1)} %all-gather.5.cloned.1.call-done, f32[128,8,4096]{2,0,1:T(8,128)} %get-tuple-element.20, f32[128,8]{0,1:T(8,128)S(1)} %broadcast_maximum_fusion, f32[128,8]{0,1:T(8,128)S(1)} %fusion), kind=kOutput, calls=%fused_computation.19 | convolution fusion | flops 1623392256 | bytes 19144704 | tf_op jit(solution)/shard_map/qhk,kv->qhv/dot_general | solution.py:43
  203.6 2.7 fusion.22
  206.4 0.1 stack.38
  206.5 93.2 %psum.7 = f32[5,1536]{1,0:T(8,128)S(1)} all-reduce(f32[5,1536]{1,0:T(8,128)S(1)} %stack.38), channel_id=1, replica_groups=mesh['dp'=16,'ctx'=32] {'dp','ctx'}, use_global_device_ids=true, to_apply=%region_7.0 | all-reduce | flops 7680 | bytes 61440 | tf_op jit(solution)/shard_map/psum | solution.py:69
  299.7 0.2 fusion.31
  299.9 6.2 %collective-permute-start.2 = (bf16[1,1,1536]{1,2,0:T(8,128)(2,1)S(1)}, bf16[1,1,1536]{1,2,0:T(8,128)(2,1)S(1)}, u32[]{:S(2)}, u32[]{:S(2)}) collective-permute-start(bf16[1,1,1536]{1,2,0:T(8,128)(2,1)S(1)} %get-tuple-element.17), channel_id=1, source_target_pairs={{0,1},{1,2},{2,3},{3,4},{4,5},{5,6},{6,7},{7,8},{8,9},{9,10},{10,1... | collective-permute-start | bytes 9224 | tf_op jit(solution)/shard_map/ppermute | solution.py:19
  306.1 1.9 collective-permute-start.3
  308.0 0.6 broadcast_multiply_fusion
  308.6 11.6 %collective-permute-done.2 = bf16[1,1,1536]{1,2,0:T(8,128)(2,1)S(1)} collective-permute-done((bf16[1,1,1536]{1,2,0:T(8,128)(2,1)S(1)}, bf16[1,1,1536]{1,2,0:T(8,128)(2,1)S(1)}, u32[]{:S(2)}, u32[]{:S(2)}) %collective-permute-start.2) | collective-permute-done | bytes 3104 | tf_op jit(solution)/shard_map/ppermute | solution.py:19
  320.2 10.3 %collective-permute-done.3 = bf16[1,1,1536]{1,2,0:T(8,128)(2,1)S(1)} collective-permute-done((bf16[1,1,1536]{1,2,0:T(8,128)(2,1)S(1)}, bf16[1,1,1536]{1,2,0:T(8,128)(2,1)S(1)}, u32[]{:S(2)}, u32[]{:S(2)}) %collective-permute-start.3) | collective-permute-done | bytes 3104 | tf_op jit(solution)/shard_map/ppermute | solution.py:21
  330.5 0.4 maximum_convert_fusion
  330.9 1.7 fusion.26
  332.6 0.1 pad_maximum_fusion.1
  332.7 0.8 copy.30
  333.5 1.2 convert_element_type.56
  (15 shorter events, 0.1 us)
Async XLA Ops:
  7.2 141.6 %all-gather.3.cloned.1.call-start = ((), (), s32[]{:S(2)}) async-start(), calls=%async_computation.2 | async-start | bytes 1081344 | tf_op jit(solution)/shard_map/all_gather | solution.py:35
  20.2 37.0 %copy-start.1 = (bf16[1,256,1536]{2,1,0:T(8,128)(2,1)S(1)}, bf16[1,256,1536]{2,1,0:T(8,128)(2,1)}, u32[]{:S(2)}) copy-start(bf16[1,256,1536]{2,1,0:T(8,128)(2,1)} %param.9) | copy-start | bytes 2359300
  20.2 27.4 %all-to-all-start = ((bf16[32,2,3072]{2,1,0:T(2,128)(2,1)}), bf16[32,2,3072]{2,1,0:T(2,128)(2,1)S(1)}, u32[]{:S(2)}, u32[]{:S(2)}) async-start(bf16[32,2,3072]{2,1,0:T(2,128)(2,1)} %reshape.84), calls=%async_computation | async-start | bytes 786432 | tf_op jit(solution)/shard_map/all_to_all | solution.py:52
  34.0 161.6 %all-gather.5.cloned.1.call-start = ((), (), s32[]{:S(2)}) async-start(), calls=%async_computation.3 | async-start | bytes 1622016 | tf_op jit(solution)/shard_map/all_gather | solution.py:36
  34.8 30.6 %copy-start.2 = (f32[5,1536]{1,0:T(8,128)S(1)}, f32[5,1536]{1,0:T(8,128)}, u32[]{:S(2)}) copy-start(f32[5,1536]{1,0:T(8,128)} %param.11) | copy-start | bytes 92164
  48.7 98.6 %all-to-all-start.1 = ((bf16[32,128,48]{1,2,0:T(8,128)(2,1)}), bf16[32,128,48]{1,2,0:T(8,128)(2,1)S(1)}, u32[]{:S(2)}, u32[]{:S(2)}) async-start(bf16[32,128,48]{1,2,0:T(8,128)(2,1)} %rev.6), calls=%async_computation.1 | async-start | bytes 786432 | tf_op jit(solution)/shard_map/all_to_all | solution.py:54
  57.5 23.6 %collective-permute-start = (bf16[1,2,1536]{1,2,0:T(8,128)(2,1)S(1)}, bf16[1,2,1536]{1,2,0:T(8,128)(2,1)}, u32[]{:S(2)}, u32[]{:S(2)}) collective-permute-start(bf16[1,2,1536]{1,2,0:T(8,128)(2,1)S(1)} %copy.24), channel_id=1, source_target_pairs={{0,1},{1,2},{2,3},{3,4},{4,5},{5,6},{6,7},{7,8},{8,9},{9,10},{10,1... | collective-permute-start | bytes 18440 | tf_op jit(solution)/shard_map/ppermute | solution.py:19
  63.3 23.8 %collective-permute-start.1 = (bf16[1,2,1536]{1,2,0:T(8,128)(2,1)S(1)}, bf16[1,2,1536]{1,2,0:T(8,128)(2,1)}, u32[]{:S(2)}, u32[]{:S(2)}) collective-permute-start(bf16[1,2,1536]{1,2,0:T(8,128)(2,1)S(1)} %copy.25), channel_id=1, source_target_pairs={{1,0},{2,1},{3,2},{4,3},{5,4},{6,5},{7,6},{8,7},{9,8},{10,9},{11,1... | collective-permute-start | bytes 18440 | tf_op jit(solution)/shard_map/ppermute | solution.py:21
  166.7 36.9 %copy-start = (bf16[1,128,1536]{1,2,0:T(8,128)(2,1)S(1)}, bf16[1,128,1536]{1,2,0:T(8,128)(2,1)}, u32[]{:S(2)}) copy-start(bf16[1,128,1536]{1,2,0:T(8,128)(2,1)} %slice.69) | copy-start | bytes 1179652
  299.9 20.3 %collective-permute-start.2 = (bf16[1,1,1536]{1,2,0:T(8,128)(2,1)S(1)}, bf16[1,1,1536]{1,2,0:T(8,128)(2,1)S(1)}, u32[]{:S(2)}, u32[]{:S(2)}) collective-permute-start(bf16[1,1,1536]{1,2,0:T(8,128)(2,1)S(1)} %get-tuple-element.17), channel_id=1, source_target_pairs={{0,1},{1,2},{2,3},{3,4},{4,5},{5,6},{6,7},{7,8},{8,9},{9,10},{10,1... | collective-permute-start | bytes 9224 | tf_op jit(solution)/shard_map/ppermute | solution.py:19
  306.1 24.4 %collective-permute-start.3 = (bf16[1,1,1536]{1,2,0:T(8,128)(2,1)S(1)}, bf16[1,1,1536]{1,2,0:T(8,128)(2,1)S(1)}, u32[]{:S(2)}, u32[]{:S(2)}) collective-permute-start(bf16[1,1,1536]{1,2,0:T(8,128)(2,1)S(1)} %get-tuple-element.18), channel_id=1, source_target_pairs={{1,0},{2,1},{3,2},{4,3},{5,4},{6,5},{7,6},{8,7},{9,8},{10,9},{11,1... | collective-permute-start | bytes 9224 | tf_op jit(solution)/shard_map/ppermute | solution.py:21
Sparse Core Ops, SparseCore 0:
  11.2 102.2 all-gather.2
  116.5 79.0 all-gather.4
where the time goes:
time: 342 us; the launch traced here: 341 us
  blocking collectives  93.2 us (27%)
  local copies, waits for them, and re-layouts  82.9 us (24%)
  waiting for transfers between devices  70.9 us (21%)
  starting transfers between devices  38.1 us (11%)
  other arithmetic  24.9 us (7%)
  matrix products  17.2 us (5%)
  between operations  14.3 us (4%)
    psum x1, blocking collectives, body(): summed = lax.psum(partial_grad, ('dp', 'ctx'))  93.2 us
    slice x5, local copies, waits for them, and re-layouts, body(): padded[:, k:k + 2 * tok_rows:2, :].astype(jnp.float32)  72.8 us
    all_gather x1, waiting for transfers between devices, body(): value_piece = lax.all_gather(values, 'ctx', axis=1, tiled=True)  29 us
    ppermute x2, waiting for transfers between devices, padded_2(): lax.ppermute(head, axis, [((i + 1) % count, i) for i in range(ends)])  16.2 us
    all_to_all x1, starting transfers between devices, body(): lax.all_to_all(rc_state, 'ctx', split_axis=2, concat_axis=0, tiled=True)  13.8 us
    all_to_all x1, waiting for transfers between devices, body(): lax.all_to_all(rc_state, 'ctx', split_axis=2, concat_axis=0, tiled=True)  12.8 us
    ppermute x2, starting transfers between devices, padded_2(): lax.ppermute(tail, axis, [(i, (i + 1) % count) for i in range(ends)])  11.7 us
    ppermute x2, waiting for transfers between devices, padded_2(): lax.ppermute(tail, axis, [(i, (i + 1) % count) for i in range(ends)])  11.6 us
  transfers between devices with their start and end apart: 8, of which 5 were waited for; matrix products, arithmetic and copies ran while one was open for 32% of the time, Pallas kernels for 0%

commit v1 on v0

--- a/solution.py
+++ b/solution.py
@@ -49,7 +49,9 @@
     coarse = conv_weight[0] * taps[0]
     for k in range(1, KW):
         coarse = coarse + conv_weight[k] * taps[k]
-    slices = lax.all_to_all(rc_state, "ctx", split_axis=2, concat_axis=0, tiled=True)
+    parts = jnp.split(rc_state, lax.axis_size("ctx"), axis=2)
+    arrived = lax.all_to_all(jnp.stack(parts), "ctx", 0, 0)
+    slices = jnp.concatenate(arrived, axis=0)
     flipped = slices[::-1]
     mirrored = lax.all_to_all(flipped, "ctx", split_axis=0, concat_axis=2, tiled=True)
     grad = coarse + attended - mirrored[:, ::-1, :].astype(jnp.float32)

time: 342 us -> 354 us (1.035)
  local copies, waits for them, and re-layouts: 82.9 us -> 103 us
  other arithmetic: 24.9 us -> 16.1 us
    unnamed x13 -> x73, local copies, waits for them, and re-layouts: 5.16 us -> 22 us
    unnamed x1 -> x0, other arithmetic: 8.8 us -> none
  transfers between devices with their start and end apart: 8 -> 8, of which waited for: 5 -> 5; matrix products, arithmetic and copies ran while one was open for 32% -> 34% of each run, Pallas kernels for 0% -> 0%
where the time goes in v1:
time: 354 us; the launch traced here: 353 us
  local copies, waits for them, and re-layouts  103 us (29%)
  blocking collectives  93.2 us (26%)
  waiting for transfers between devices  71.3 us (20%)
  starting transfers between devices  38 us (11%)
  matrix products  17.2 us (5%)
  other arithmetic  16.1 us (5%)
  between operations  14.4 us (4%)
    psum x1, blocking collectives, body(): summed = lax.psum(partial_grad, ('dp', 'ctx'))  93.2 us
    slice x5, local copies, waits for them, and re-layouts, body(): padded[:, k:k + 2 * tok_rows:2, :].astype(jnp.float32)  72.8 us
    all_gather x1, waiting for transfers between devices, body(): value_piece = lax.all_gather(values, 'ctx', axis=1, tiled=True)  28.2 us
    unnamed x73, local copies, waits for them, and re-layouts  22 us
    ppermute x2, waiting for transfers between devices, padded_2(): lax.ppermute(head, axis, [((i + 1) % count, i) for i in range(ends)])  17.4 us
    all_to_all x1, starting transfers between devices, body(): arrived = lax.all_to_all(jnp.stack(parts), 'ctx', 0, 0)  13.8 us
    all_to_all x1, waiting for transfers between devices, body(): arrived = lax.all_to_all(jnp.stack(parts), 'ctx', 0, 0)  12.7 us
    ppermute x2, starting transfers between devices, padded_2(): lax.ppermute(tail, axis, [(i, (i + 1) % count) for i in range(ends)])  11.7 us
  transfers between devices with their start and end apart: 8, of which 5 were waited for; matrix products, arithmetic and copies ran while one was open for 34% of the time, Pallas kernels for 0%

profile of v1, /device:TPU:184, one launch (start us, length us, event | category | flops | bytes accessed | tf_op | source)
XLA Modules:
  0.0 353.5 jit_solution(1659261509632477971)
XLA Ops:
  7.2 0.7 all-gather.3.cloned.1.call-update
  7.9 1.4 fusion.33
  9.3 1.5 fusion.32
  10.9 0.6 constant_dynamic-update-slice_fusion.31
  13.8 0.6 constant_dynamic-update-slice_fusion.30
  14.4 0.6 constant_dynamic-update-slice_fusion.29
  15.0 0.6 constant_dynamic-update-slice_fusion.28
  15.6 0.6 constant_dynamic-update-slice_fusion.27
  16.2 0.6 constant_dynamic-update-slice_fusion.26
  16.8 0.6 constant_dynamic-update-slice_fusion.25
  17.4 0.6 constant_dynamic-update-slice_fusion.24
  18.0 0.6 constant_dynamic-update-slice_fusion.23
  19.9 0.6 constant_dynamic-update-slice_fusion.20
  21.7 0.6 constant_dynamic-update-slice_fusion.17
  23.5 0.6 constant_dynamic-update-slice_fusion.14
  24.7 0.6 constant_dynamic-update-slice_fusion.12
  26.5 0.6 constant_dynamic-update-slice_fusion.9
  28.9 0.6 constant_dynamic-update-slice_fusion.6
  30.1 0.6 constant_dynamic-update-slice_fusion.4
  33.2 13.8 %all-to-all-start = ((bf16[32,1,128,48]{2,3,1,0:T(8,128)(2,1)}), bf16[32,1,128,48]{2,3,1,0:T(8,128)(2,1)S(1)}, u32[]{:S(2)}, u32[]{:S(2)}) async-start(bf16[32,1,128,48]{2,3,1,0:T(8,128)(2,1)} %constant_dynamic-update-slice_fusion), calls=%async_computation | async-start | bytes 786432 | tf_op jit(solution)/shard_map/all_to_all | solution.py:53
  47.0 0.7 all-gather.5.cloned.1.call-update
  47.7 12.7 %all-to-all-done = bf16[32,1,128,48]{2,3,1,0:T(8,128)(2,1)S(1)} async-done(((bf16[32,1,128,48]{2,3,1,0:T(8,128)(2,1)}), bf16[32,1,128,48]{2,3,1,0:T(8,128)(2,1)S(1)}, u32[]{:S(2)}, u32[]{:S(2)}) %all-to-all-start) | async-done | bytes 393248 | tf_op jit(solution)/shard_map/all_to_all | solution.py:53
  60.4 0.8 rev.6
  61.2 8.4 %all-to-all-start.1 = ((bf16[32,128,48]{1,2,0:T(8,128)(2,1)}), bf16[32,128,48]{1,2,0:T(8,128)(2,1)S(1)}, u32[]{:S(2)}, u32[]{:S(2)}) async-start(bf16[32,128,48]{1,2,0:T(8,128)(2,1)} %rev.6), calls=%async_computation.1 | async-start | bytes 786432 | tf_op jit(solution)/shard_map/all_to_all | solution.py:56
  69.9 5.5 %collective-permute-start = (bf16[1,2,1536]{1,2,0:T(8,128)(2,1)S(1)}, bf16[1,2,1536]{1,2,0:T(8,128)(2,1)}, u32[]{:S(2)}, u32[]{:S(2)}) collective-permute-start(bf16[1,2,1536]{1,2,0:T(8,128)(2,1)S(1)} %copy.86), channel_id=1, source_target_pairs={{0,1},{1,2},{2,3},{3,4},{4,5},{5,6},{6,7},{7,8},{8,9},{9,10},{10,1... | collective-permute-start | bytes 18440 | tf_op jit(solution)/shard_map/ppermute | solution.py:19
  75.6 2.1 collective-permute-start.1
  78.2 14.4 %slice.65 = bf16[1,128,1536]{1,2,0:T(8,128)(2,1)S(1)} slice(bf16[1,256,1536]{1,2,0:T(8,128)(2,1)S(1)} %copy.88), slice={[0:1:1], [0:256:2], [0:1536:1]} | slice | bytes 786432 | tf_op jit(solution)/shard_map/slice | solution.py:48
  92.6 7.1 %collective-permute-done.1 = bf16[1,2,1536]{1,2,0:T(8,128)(2,1)} collective-permute-done((bf16[1,2,1536]{1,2,0:T(8,128)(2,1)S(1)}, bf16[1,2,1536]{1,2,0:T(8,128)(2,1)}, u32[]{:S(2)}, u32[]{:S(2)}) %collective-permute-start.1) | collective-permute-done | bytes 6176 | tf_op jit(solution)/shard_map/ppermute | solution.py:21
  99.7 1.8 pad_maximum_fusion
  101.6 14.4 %slice.61 = bf16[1,128,1536]{1,2,0:T(8,128)(2,1)S(1)} slice(bf16[1,260,1536]{1,2,0:T(8,128)(2,1)S(1)} %pad_maximum_fusion), slice={[0:1:1], [0:256:2], [0:1536:1]} | slice | bytes 786432 | tf_op jit(solution)/shard_map/slice | solution.py:48
  116.0 14.4 %slice.63 = bf16[1,128,1536]{1,2,0:T(8,128)(2,1)S(1)} slice(bf16[1,260,1536]{1,2,0:T(8,128)(2,1)S(1)} %pad_maximum_fusion), slice={[0:1:1], [1:257:2], [0:1536:1]} | slice | bytes 786432 | tf_op jit(solution)/shard_map/slice | solution.py:48
  130.4 14.7 %slice.67 = bf16[1,128,1536]{1,2,0:T(8,128)(2,1)S(1)} slice(bf16[1,260,1536]{1,2,0:T(8,128)(2,1)S(1)} %pad_maximum_fusion), slice={[0:1:1], [3:259:2], [0:1536:1]} | slice | bytes 786432 | tf_op jit(solution)/shard_map/slice | solution.py:48
  145.1 15.0 %slice.69 = bf16[1,128,1536]{1,2,0:T(8,128)(2,1)} slice(bf16[1,260,1536]{1,2,0:T(8,128)(2,1)S(1)} %pad_maximum_fusion), slice={[0:1:1], [4:260:2], [0:1536:1]} | slice | bytes 786432 | tf_op jit(solution)/shard_map/slice | solution.py:48
  160.1 1.3 rev.7
  161.4 9.3 %multiply_reduce_fusion = (f32[128,8]{0,1:T(8,128)S(1)}, f32[128,8,4096]{2,0,1:T(8,128)}) fusion(bf16[1,4096,128]{2,1,0:T(8,128)(2,1)} %all-gather.3.cloned.1.call-done, bf16[128,8,128]{2,1,0:T(8,128)(2,1)S(1)} %bitcast.92), kind=kOutput, calls=%fused_computation.1 | convolution fusion | flops 1082129408 | bytes 18092032 | tf_op jit(solution)/shard_map/qhd,kd->qhk/dot_general | solution.py:37
  170.7 8.7 %fusion = f32[128,8]{0,1:T(8,128)S(1)} fusion(f32[128,8,4096]{2,0,1:T(8,128)} %get-tuple-element.52, f32[128,8]{0,1:T(8,128)S(1)} %broadcast_maximum_fusion), kind=kLoop, calls=%fused_computation.2 | loop fusion | flops 12581888 | bytes 16785408 | tf_op jit(solution)/shard_map/reduce_sum | solution.py:42
  179.4 28.2 %all-gather.5.cloned.1.call-done = bf16[1,4096,192]{1,2,0:T(8,128)(2,1)} async-done(((bf16[1,128,192]{1,2,0:T(8,128)(2,1)}), bf16[1,4096,192]{1,2,0:T(8,128)(2,1)}) %all-gather.5.cloned.1.call-update) | async-done | bytes 1572880 | tf_op jit(solution)/shard_map/all_gather | solution.py:36
  207.6 8.0 %fusion.7 = f32[128,8,192]{0,2,1:T(8,128)S(1)} fusion(bf16[1,4096,192]{1,2,0:T(8,128)(2,1)} %all-gather.5.cloned.1.call-done, f32[128,8,4096]{2,0,1:T(8,128)} %get-tuple-element.52, f32[128,8]{0,1:T(8,128)S(1)} %broadcast_maximum_fusion, f32[128,8]{0,1:T(8,128)S(1)} %fusion), kind=kOutput, calls=%fused_computation.19 | convolution fusion | flops 1623392256 | bytes 19144704 | tf_op jit(solution)/shard_map/qhk,kv->qhv/dot_general | solution.py:43
  215.6 2.7 fusion.22
  218.5 93.2 %psum.7 = f32[5,1536]{1,0:T(8,128)S(1)} all-reduce(f32[5,1536]{1,0:T(8,128)S(1)} %stack.170), channel_id=1, replica_groups=mesh['dp'=16,'ctx'=32] {'dp','ctx'}, use_global_device_ids=true, to_apply=%region_7.0 | all-reduce | flops 7680 | bytes 61440 | tf_op jit(solution)/shard_map/psum | solution.py:71
  311.9 6.2 %collective-permute-start.2 = (bf16[1,1,1536]{1,2,0:T(8,128)(2,1)S(1)}, bf16[1,1,1536]{1,2,0:T(8,128)(2,1)S(1)}, u32[]{:S(2)}, u32[]{:S(2)}) collective-permute-start(bf16[1,1,1536]{1,2,0:T(8,128)(2,1)S(1)} %get-tuple-element.17), channel_id=1, source_target_pairs={{0,1},{1,2},{2,3},{3,4},{4,5},{5,6},{6,7},{7,8},{8,9},{9,10},{10,1... | collective-permute-start | bytes 9224 | tf_op jit(solution)/shard_map/ppermute | solution.py:19
  318.1 1.9 collective-permute-start.3
  320.0 0.6 broadcast_multiply_fusion
  320.6 11.6 %collective-permute-done.2 = bf16[1,1,1536]{1,2,0:T(8,128)(2,1)S(1)} collective-permute-done((bf16[1,1,1536]{1,2,0:T(8,128)(2,1)S(1)}, bf16[1,1,1536]{1,2,0:T(8,128)(2,1)S(1)}, u32[]{:S(2)}, u32[]{:S(2)}) %collective-permute-start.2) | collective-permute-done | bytes 3104 | tf_op jit(solution)/shard_map/ppermute | solution.py:19
  332.2 10.3 %collective-permute-done.3 = bf16[1,1,1536]{1,2,0:T(8,128)(2,1)S(1)} collective-permute-done((bf16[1,1,1536]{1,2,0:T(8,128)(2,1)S(1)}, bf16[1,1,1536]{1,2,0:T(8,128)(2,1)S(1)}, u32[]{:S(2)}, u32[]{:S(2)}) %collective-permute-start.3) | collective-permute-done | bytes 3104 | tf_op jit(solution)/shard_map/ppermute | solution.py:21
  342.9 1.7 fusion.26
  344.7 0.8 copy.123
  345.5 1.2 convert_element_type.56
  (77 shorter events, 14.4 us)
Async XLA Ops:
  7.2 154.2 %all-gather.3.cloned.1.call-start = ((), (), s32[]{:S(2)}) async-start(), calls=%async_computation.2 | async-start | bytes 1081344 | tf_op jit(solution)/shard_map/all_gather | solution.py:35
  10.8 58.8 %copy-start.1 = (bf16[1,256,1536]{2,1,0:T(8,128)(2,1)S(1)}, bf16[1,256,1536]{2,1,0:T(8,128)(2,1)}, u32[]{:S(2)}) copy-start(bf16[1,256,1536]{2,1,0:T(8,128)(2,1)} %param.9) | copy-start | bytes 2359300
  13.0 64.7 %copy-start.3 = (f32[5,1536]{1,0:T(8,128)S(1)}, f32[5,1536]{1,0:T(8,128)}, u32[]{:S(2)}) copy-start(f32[5,1536]{1,0:T(8,128)} %param.11) | copy-start | bytes 92164
  33.2 45.0 %copy-start.2 = (bf16[1,128,1024]{2,1,0:T(8,128)(2,1)S(1)}, bf16[1,128,1024]{2,1,0:T(8,128)(2,1)}, u32[]{:S(2)}) copy-start(bf16[1,128,1024]{2,1,0:T(8,128)(2,1)} %param.6) | copy-start | bytes 786436
  33.2 27.3 %all-to-all-start = ((bf16[32,1,128,48]{2,3,1,0:T(8,128)(2,1)}), bf16[32,1,128,48]{2,3,1,0:T(8,128)(2,1)S(1)}, u32[]{:S(2)}, u32[]{:S(2)}) async-start(bf16[32,1,128,48]{2,3,1,0:T(8,128)(2,1)} %constant_dynamic-update-slice_fusion), calls=%async_computation | async-start | bytes 786432 | tf_op jit(solution)/shard_map/all_to_all | solution.py:53
  47.0 160.7 %all-gather.5.cloned.1.call-start = ((), (), s32[]{:S(2)}) async-start(), calls=%async_computation.3 | async-start | bytes 1622016 | tf_op jit(solution)/shard_map/all_gather | solution.py:36
  61.2 98.9 %all-to-all-start.1 = ((bf16[32,128,48]{1,2,0:T(8,128)(2,1)}), bf16[32,128,48]{1,2,0:T(8,128)(2,1)S(1)}, u32[]{:S(2)}, u32[]{:S(2)}) async-start(bf16[32,128,48]{1,2,0:T(8,128)(2,1)} %rev.6), calls=%async_computation.1 | async-start | bytes 786432 | tf_op jit(solution)/shard_map/all_to_all | solution.py:56
  69.9 22.7 %collective-permute-start = (bf16[1,2,1536]{1,2,0:T(8,128)(2,1)S(1)}, bf16[1,2,1536]{1,2,0:T(8,128)(2,1)}, u32[]{:S(2)}, u32[]{:S(2)}) collective-permute-start(bf16[1,2,1536]{1,2,0:T(8,128)(2,1)S(1)} %copy.86), channel_id=1, source_target_pairs={{0,1},{1,2},{2,3},{3,4},{4,5},{5,6},{6,7},{7,8},{8,9},{9,10},{10,1... | collective-permute-start | bytes 18440 | tf_op jit(solution)/shard_map/ppermute | solution.py:19
  75.6 24.1 %collective-permute-start.1 = (bf16[1,2,1536]{1,2,0:T(8,128)(2,1)S(1)}, bf16[1,2,1536]{1,2,0:T(8,128)(2,1)}, u32[]{:S(2)}, u32[]{:S(2)}) collective-permute-start(bf16[1,2,1536]{1,2,0:T(8,128)(2,1)S(1)} %copy.87), channel_id=1, source_target_pairs={{1,0},{2,1},{3,2},{4,3},{5,4},{6,5},{7,6},{8,7},{9,8},{10,9},{11,1... | collective-permute-start | bytes 18440 | tf_op jit(solution)/shard_map/ppermute | solution.py:21
  179.4 36.2 %copy-start = (bf16[1,128,1536]{1,2,0:T(8,128)(2,1)S(1)}, bf16[1,128,1536]{1,2,0:T(8,128)(2,1)}, u32[]{:S(2)}) copy-start(bf16[1,128,1536]{1,2,0:T(8,128)(2,1)} %slice.69) | copy-start | bytes 1179652
  311.9 20.3 %collective-permute-start.2 = (bf16[1,1,1536]{1,2,0:T(8,128)(2,1)S(1)}, bf16[1,1,1536]{1,2,0:T(8,128)(2,1)S(1)}, u32[]{:S(2)}, u32[]{:S(2)}) collective-permute-start(bf16[1,1,1536]{1,2,0:T(8,128)(2,1)S(1)} %get-tuple-element.17), channel_id=1, source_target_pairs={{0,1},{1,2},{2,3},{3,4},{4,5},{5,6},{6,7},{7,8},{8,9},{9,10},{10,1... | collective-permute-start | bytes 9224 | tf_op jit(solution)/shard_map/ppermute | solution.py:19
  318.1 24.4 %collective-permute-start.3 = (bf16[1,1,1536]{1,2,0:T(8,128)(2,1)S(1)}, bf16[1,1,1536]{1,2,0:T(8,128)(2,1)S(1)}, u32[]{:S(2)}, u32[]{:S(2)}) collective-permute-start(bf16[1,1,1536]{1,2,0:T(8,128)(2,1)S(1)} %get-tuple-element.18), channel_id=1, source_target_pairs={{1,0},{2,1},{3,2},{4,3},{5,4},{6,5},{7,6},{8,7},{9,8},{10,9},{11,1... | collective-permute-start | bytes 9224 | tf_op jit(solution)/shard_map/ppermute | solution.py:21
Sparse Core Ops, SparseCore 0:
  11.2 110.4 all-gather.2
  124.7 82.8 all-gather.4
